TPU v7x, 32 devices: a whole 2x2x4 slice. The times are simulated.
32 devices in a mesh: dp: 2 (over x), seq: 16 (over z, y, core).
Axes of the slice: x: 2, y: 2, z: 4, core: 2. Of those that a mesh axis runs over, the one named last changes fastest.
Arguments:
- hidden_in: bfloat16 [2, 2, 1024, 2048], P(None, 'dp', 'seq'), may hold values from -6 to 6
- cotangent: bfloat16 [2, 2, 1024, 2048], P(None, 'dp', 'seq'), may hold values from -6 to 6
- prefix_len: int32 [2, 2], P(None, 'dp'), may hold values from 102 to 512
- qkv_weight: bfloat16 [6144, 2048], P(('dp', 'seq')), may hold values from -0.125 to 0.125
- dense_weight: bfloat16 [2048, 2048], P(('dp', 'seq')), may hold values from -2 to 2
- fc1_weight: bfloat16 [8192, 2048], P(('dp', 'seq')), may hold values from -0.125 to 0.125
- fc2_weight: bfloat16 [8192, 2048], P(('dp', 'seq')), may hold values from -0.0625 to 0.0625
- norm_gain: bfloat16 [2048], P(('dp', 'seq')), may hold values from 0.5 to 1.5
- norm_shift: bfloat16 [2048], P(('dp', 'seq')), may hold values from -3 to 3
- qkv_bias: bfloat16 [6144], P(('dp', 'seq')), may hold values from -3 to 3
- dense_bias: bfloat16 [2048], P(('dp', 'seq')), may hold values from -3 to 3
- fc1_bias: bfloat16 [8192], P(('dp', 'seq')), may hold values from -3 to 3
- fc2_bias: bfloat16 [2048], P(('dp', 'seq')), may hold values from -3 to 3
Outputs:
- hidden_out: bfloat16 [2, 2, 1024, 2048], P(None, 'dp', 'seq')
- input_grad: float32 [2, 2, 1024, 2048], P(None, 'dp', 'seq')
- qkv_weight_grad: float32 [6144, 2048], P(('dp', 'seq'))
- dense_weight_grad: float32 [2048, 2048], P(('dp', 'seq'))
- fc1_weight_grad: float32 [8192, 2048], P(('dp', 'seq'))
- fc2_weight_grad: float32 [8192, 2048], P(('dp', 'seq'))
- gain_grad: float32 [2048], P(('dp', 'seq'))
- shift_grad: float32 [2048], P(('dp', 'seq'))
- qkv_bias_grad: float32 [6144], P(('dp', 'seq'))
- dense_bias_grad: float32 [2048], P(('dp', 'seq'))
- fc1_bias_grad: float32 [8192], P(('dp', 'seq'))
- fc2_bias_grad: float32 [2048], P(('dp', 'seq'))
All inputs are finite; a program needn't handle non-finite values.
Results may differ from a plain program's by a relative error of at most 0.01.
Values may be sent and summed in bfloat16 or wider, within the bound.
A program may use at most 704 MiB of HBM per device.

v0:
```python
from functools import partial
import math

import jax
import jax.numpy as jnp
from jax import lax
from jax.sharding import PartitionSpec as P

HEADS = 32
HEAD = 64
ROT = 32


NORM_EPS = 1e-05
MASKED_LOW = -1e30
TANH_FACTOR = 0.7978845608028654
CUBIC_FACTOR = 0.044715


def gelu_tanh(inputs_in):
    return (
        0.5
        * inputs_in
        * (
            1.0
            + jnp.tanh(TANH_FACTOR * (inputs_in + CUBIC_FACTOR * inputs_in * inputs_in * inputs_in))
        )
    )


def rotary_tables(first_place, length):
    half_rot = ROT // 2
    frequency = jnp.power(10000.0, -jnp.arange(half_rot).astype(jnp.float32) * 2.0 / ROT)
    places = (first_place + jnp.arange(length, dtype=jnp.int32)).astype(jnp.float32)
    angles = places[:, None] * frequency[None, :]
    angles = jnp.concatenate([angles, angles], 1)
    return (jnp.cos(angles)[:, None, :], jnp.sin(angles)[:, None, :])


def rotate(head_view, cosine, sine):
    half_rot = ROT // 2
    turned = head_view[..., :ROT]
    swapped = jnp.concatenate([-turned[..., half_rot:], turned[..., :half_rot]], -1)
    return jnp.concatenate([turned * cosine + swapped * sine, head_view[..., ROT:]], -1)


def norm_apply(tokens, scale_gain, shift_bias):
    centred = tokens - jnp.mean(tokens, 1, keepdims=True)
    rstd = lax.rsqrt(jnp.mean(centred * centred, 1, keepdims=True) + NORM_EPS)
    return centred * rstd * scale_gain + shift_bias


def contract_last(left, right):
    return lax.dot_general(
        left, right, (((1,), (1,)), ((), ())), preferred_element_type=jnp.float32
    )


def visible_mask(query_places, key_places, limits):
    reach = jnp.maximum(query_places[None, :], limits[:, None] - 1)
    return (key_places[None, None, :] <= reach[:, :, None])[:, None]


def forward_part(tokens, limits, params, first_place, cosine, sine):
    (
        qkv_weight,
        dense_weight,
        fc1_weight,
        fc2_weight,
        norm_gain,
        norm_shift,
        qkv_bias,
        dense_bias,
        fc1_bias,
        fc2_bias,
    ) = params
    seq_count, local_len, model_width = tokens.shape
    score_scale = 1.0 / math.sqrt(HEAD)
    flat_rows = tokens.reshape(seq_count * local_len, model_width).astype(jnp.float32)
    normed_low = norm_apply(
        flat_rows, norm_gain.astype(jnp.float32), norm_shift.astype(jnp.float32)
    ).astype(jnp.bfloat16)
    merged = contract_last(normed_low, qkv_weight) + qkv_bias.astype(jnp.float32)
    head_view = merged.reshape(seq_count, local_len, 3, HEADS, HEAD)
    query_low = rotate(head_view[:, :, 0], cosine, sine).astype(jnp.bfloat16)
    key_low = (
        rotate(head_view[:, :, 1], cosine, sine)
        .astype(jnp.bfloat16)
        .reshape(seq_count, local_len, model_width)
    )
    value_low = head_view[:, :, 2].astype(jnp.bfloat16).reshape(seq_count, local_len, model_width)
    query_places = first_place + jnp.arange(local_len, dtype=jnp.int32)
    row_top = jnp.full((seq_count, HEADS, local_len), MASKED_LOW, jnp.float32)
    keys_piece = lax.all_gather(key_low, "seq", axis=1, tiled=True)
    values_piece = lax.all_gather(value_low, "seq", axis=1, tiled=True)
    piece_len = keys_piece.shape[1]
    keys_piece = keys_piece.reshape(seq_count, piece_len, HEADS, HEAD)
    values_piece = values_piece.reshape(seq_count, piece_len, HEADS, HEAD)
    scores = (
        jnp.einsum("sqhd,skhd->shqk", query_low, keys_piece, preferred_element_type=jnp.float32)
        * score_scale
    )
    visible = visible_mask(query_places, jnp.arange(piece_len, dtype=jnp.int32), limits)
    masked = jnp.where(visible, scores, MASKED_LOW)
    new_top = jnp.maximum(row_top, jnp.max(masked, -1))
    exp_weights = jnp.where(visible, jnp.exp(masked - new_top[..., None]), 0.0)
    row_total = jnp.sum(exp_weights, -1)
    accum = jnp.einsum(
        "shqk,skhd->shqd",
        exp_weights.astype(jnp.bfloat16),
        values_piece,
        preferred_element_type=jnp.float32,
    )
    row_top, row_total, accum = (new_top, row_total, accum)
    mixed = accum / row_total[..., None]
    log_total = row_top + jnp.log(row_total)
    mixed_low = (
        mixed.transpose(0, 2, 1, 3).reshape(seq_count * local_len, model_width).astype(jnp.bfloat16)
    )
    hidden_pre = contract_last(normed_low, fc1_weight) + fc1_bias.astype(jnp.float32)
    act_low = gelu_tanh(hidden_pre).astype(jnp.bfloat16)
    result = (
        flat_rows
        + jnp.dot(mixed_low, dense_weight, preferred_element_type=jnp.float32)
        + dense_bias.astype(jnp.float32)
    )
    result = (
        result
        + jnp.dot(act_low, fc2_weight, preferred_element_type=jnp.float32)
        + fc2_bias.astype(jnp.float32)
    )
    saved_parts = (
        flat_rows,
        normed_low,
        query_low,
        key_low,
        value_low,
        mixed,
        log_total,
        hidden_pre,
        act_low,
        mixed_low,
    )
    return (result.astype(jnp.bfloat16).reshape(tokens.shape), saved_parts)


def backward_part(grad_low, limits, params, first_place, cosine, sine, saved_parts):
    (
        qkv_weight,
        dense_weight,
        fc1_weight,
        fc2_weight,
        norm_gain,
        norm_shift,
        qkv_bias,
        dense_bias,
        fc1_bias,
        fc2_bias,
    ) = params
    (
        flat_rows,
        normed_low,
        query_low,
        key_low,
        value_low,
        mixed,
        log_total,
        hidden_pre,
        act_low,
        mixed_low,
    ) = saved_parts
    seq_count, local_len, model_width = grad_low.shape
    score_scale = 1.0 / math.sqrt(HEAD)
    grad_rows_low = grad_low.reshape(seq_count * local_len, model_width)
    grad_rows = grad_rows_low.astype(jnp.float32)
    grad_mixed_low = contract_last(grad_rows_low, dense_weight).astype(jnp.bfloat16)
    grad_act = contract_last(grad_rows_low, fc2_weight)
    gelu_pull = jax.vjp(gelu_tanh, hidden_pre)[1]
    grad_hidden_low = gelu_pull(grad_act)[0].astype(jnp.bfloat16)
    grad_out_heads = grad_mixed_low.reshape(seq_count, local_len, HEADS, HEAD)
    delta = jnp.sum(grad_out_heads.astype(jnp.float32).transpose(0, 2, 1, 3) * mixed, -1)
    stats_lse, stats_delta = (
        lax.all_gather(log_total.transpose(0, 2, 1), "seq", axis=1, tiled=True),
        lax.all_gather(delta.transpose(0, 2, 1), "seq", axis=1, tiled=True),
    )
    local_places = first_place + jnp.arange(local_len, dtype=jnp.int32)
    key_heads = key_low.reshape(seq_count, local_len, HEADS, HEAD)
    value_heads = value_low.reshape(seq_count, local_len, HEADS, HEAD)
    keys_piece = lax.all_gather(key_low, "seq", axis=1, tiled=True)
    values_piece = lax.all_gather(value_low, "seq", axis=1, tiled=True)
    piece_len = keys_piece.shape[1]
    keys_piece = keys_piece.reshape(seq_count, piece_len, HEADS, HEAD)
    values_piece = values_piece.reshape(seq_count, piece_len, HEADS, HEAD)
    scores = (
        jnp.einsum("sqhd,skhd->shqk", query_low, keys_piece, preferred_element_type=jnp.float32)
        * score_scale
    )
    visible = visible_mask(local_places, jnp.arange(piece_len, dtype=jnp.int32), limits)
    prob_rows = jnp.where(visible, jnp.exp(scores - log_total[..., None]), 0.0)
    grad_probs = jnp.einsum(
        "sqhd,skhd->shqk", grad_out_heads, values_piece, preferred_element_type=jnp.float32
    )
    grad_scores = (prob_rows * (grad_probs - delta[..., None])).astype(jnp.bfloat16)
    grad_query = score_scale * jnp.einsum(
        "shqk,skhd->sqhd", grad_scores, keys_piece, preferred_element_type=jnp.float32
    )
    query_flat = query_low.reshape(seq_count, local_len, model_width)
    grad_out_flat = grad_mixed_low.reshape(seq_count, local_len, model_width)
    queries_piece = lax.all_gather(query_flat, "seq", axis=1, tiled=True)
    grad_out_piece = lax.all_gather(grad_out_flat, "seq", axis=1, tiled=True)
    piece_len = queries_piece.shape[1]
    queries_piece = queries_piece.reshape(seq_count, piece_len, HEADS, HEAD)
    grad_out_piece = grad_out_piece.reshape(seq_count, piece_len, HEADS, HEAD)
    piece_lse = stats_lse.transpose(0, 2, 1)
    piece_delta = stats_delta.transpose(0, 2, 1)
    scores = (
        jnp.einsum("sqhd,skhd->shqk", queries_piece, key_heads, preferred_element_type=jnp.float32)
        * score_scale
    )
    visible = visible_mask(jnp.arange(piece_len, dtype=jnp.int32), local_places, limits)
    prob_rows = jnp.where(visible, jnp.exp(scores - piece_lse[..., None]), 0.0)
    grad_probs = jnp.einsum(
        "sqhd,skhd->shqk", grad_out_piece, value_heads, preferred_element_type=jnp.float32
    )
    grad_scores = (prob_rows * (grad_probs - piece_delta[..., None])).astype(jnp.bfloat16)
    grad_values = jnp.einsum(
        "shqk,sqhd->skhd",
        prob_rows.astype(jnp.bfloat16),
        grad_out_piece,
        preferred_element_type=jnp.float32,
    )
    grad_keys = score_scale * jnp.einsum(
        "shqk,sqhd->skhd", grad_scores, queries_piece, preferred_element_type=jnp.float32
    )
    grad_keys, grad_values = (grad_keys, grad_values)
    paired = jnp.stack([grad_query, grad_keys], 0)
    rotate_pull = jax.vjp(partial(rotate, cosine=cosine, sine=sine), paired)[1]
    unturned = rotate_pull(paired)[0]
    grad_merged_low = (
        jnp.stack([unturned[0], unturned[1], grad_values], 2)
        .reshape(seq_count * local_len, 3 * model_width)
        .astype(jnp.bfloat16)
    )
    grad_normed = jnp.dot(
        grad_merged_low, qkv_weight, preferred_element_type=jnp.float32
    ) + jnp.dot(grad_hidden_low, fc1_weight, preferred_element_type=jnp.float32)
    norm_pull = jax.vjp(
        norm_apply, flat_rows, norm_gain.astype(jnp.float32), norm_shift.astype(jnp.float32)
    )[1]
    grad_flat, grad_gain, grad_shift = norm_pull(grad_normed)
    input_grad = (grad_rows + grad_flat).reshape(seq_count, local_len, model_width)
    bias_sums = jnp.sum(grad_rows, 0)
    small_terms = (
        grad_gain,
        grad_shift,
        jnp.sum(grad_merged_low.astype(jnp.float32), 0),
        bias_sums,
        jnp.sum(grad_hidden_low.astype(jnp.float32), 0),
        bias_sums,
    )
    operand_set = (normed_low, grad_merged_low, mixed_low, grad_rows_low, grad_hidden_low, act_low)
    return (input_grad, small_terms, operand_set)


def terms_builder(operand_set, row_sizes, model_width, row_count):
    normed_all, grad_merged_all, mixed_all, grad_out_all, grad_hidden_all, act_all = operand_set
    rows_qkv, rows_dense, rows_fc1, rows_fc2 = row_sizes
    block_rows = rows_qkv + rows_dense + rows_fc1 + rows_fc2
    block_count = row_count // block_rows

    def outer_term(left, right, block_width):
        term = lax.dot_general(
            left, right, (((0,), (0,)), ((), ())), preferred_element_type=jnp.float32
        )
        return term.reshape(block_count, block_width, model_width)

    term_parts = [
        outer_term(grad_merged_all, normed_all, rows_qkv),
        outer_term(mixed_all, grad_out_all, rows_dense),
        outer_term(grad_hidden_all, normed_all, rows_fc1),
        outer_term(act_all, grad_out_all, rows_fc2),
    ]
    return jnp.concatenate(term_parts, 1).reshape(row_count, model_width)


def on_device(
    hidden_in,
    cotangent,
    prefix_len,
    qkv_weight,
    dense_weight,
    fc1_weight,
    fc2_weight,
    norm_gain,
    norm_shift,
    qkv_bias,
    dense_bias,
    fc1_bias,
    fc2_bias,
):
    micro_count, seq_count, local_len, model_width = hidden_in.shape
    first_place = lax.axis_index("seq") * local_len
    cosine, sine = rotary_tables(first_place, local_len)
    row_sizes = (
        qkv_weight.shape[0],
        dense_weight.shape[0],
        fc1_weight.shape[0],
        fc2_weight.shape[0],
    )
    block_rows = row_sizes[0] + row_sizes[1] + row_sizes[2] + row_sizes[3]
    params = (
        lax.all_gather(qkv_weight, ("dp", "seq"), axis=0, tiled=True),
        lax.all_gather(dense_weight, ("dp", "seq"), axis=0, tiled=True),
        lax.all_gather(fc1_weight, ("dp", "seq"), axis=0, tiled=True),
        lax.all_gather(fc2_weight, ("dp", "seq"), axis=0, tiled=True),
        lax.all_gather(norm_gain, ("dp", "seq"), axis=0, tiled=True),
        lax.all_gather(norm_shift, ("dp", "seq"), axis=0, tiled=True),
        lax.all_gather(qkv_bias, ("dp", "seq"), axis=0, tiled=True),
        lax.all_gather(dense_bias, ("dp", "seq"), axis=0, tiled=True),
        lax.all_gather(fc1_bias, ("dp", "seq"), axis=0, tiled=True),
        lax.all_gather(fc2_bias, ("dp", "seq"), axis=0, tiled=True),
    )
    outputs = []
    input_grads = []
    small_totals = None
    operand_lists = []
    weight_rows = None
    for batch_index in range(micro_count):
        limits = prefix_len[batch_index]
        result, saved_parts = forward_part(
            hidden_in[batch_index], limits, params, first_place, cosine, sine
        )
        input_grad, small_terms, operand_set = backward_part(
            cotangent[batch_index], limits, params, first_place, cosine, sine, saved_parts
        )
        outputs.append(result)
        input_grads.append(input_grad)
        operand_lists.append(operand_set)
        if small_totals is None:
            small_totals = small_terms
        else:
            small_totals = tuple(
                (old_sum + new_term for old_sum, new_term in zip(small_totals, small_terms))
            )
    joined_set = tuple(
        (jnp.concatenate([entry[place] for entry in operand_lists], 0) for place in range(6))
    )
    weight_rows = lax.psum_scatter(
        terms_builder(
            joined_set, row_sizes, model_width, block_rows * lax.axis_size(("dp", "seq"))
        ),
        ("dp", "seq"),
        scatter_dimension=0,
        tiled=True,
    )
    rows_qkv, rows_dense, rows_fc1, rows_fc2 = row_sizes
    qkv_grad = weight_rows[:rows_qkv]
    dense_grad = weight_rows[rows_qkv : rows_qkv + rows_dense]
    fc1_grad = weight_rows[rows_qkv + rows_dense : rows_qkv + rows_dense + rows_fc1]
    fc2_grad = weight_rows[rows_qkv + rows_dense + rows_fc1 :]
    gain_grad, shift_grad, qkv_bias_grad, dense_bias_grad, fc1_bias_grad, fc2_bias_grad = (
        lax.psum_scatter(small_totals[0], ("dp", "seq"), scatter_dimension=0, tiled=True),
        lax.psum_scatter(small_totals[1], ("dp", "seq"), scatter_dimension=0, tiled=True),
        lax.psum_scatter(small_totals[2], ("dp", "seq"), scatter_dimension=0, tiled=True),
        lax.psum_scatter(small_totals[3], ("dp", "seq"), scatter_dimension=0, tiled=True),
        lax.psum_scatter(small_totals[4], ("dp", "seq"), scatter_dimension=0, tiled=True),
        lax.psum_scatter(small_totals[5], ("dp", "seq"), scatter_dimension=0, tiled=True),
    )
    return (
        jnp.stack(outputs, 0),
        jnp.stack(input_grads, 0),
        qkv_grad,
        dense_grad,
        fc1_grad,
        fc2_grad,
        gain_grad,
        shift_grad,
        qkv_bias_grad,
        dense_bias_grad,
        fc1_bias_grad,
        fc2_bias_grad,
    )


def solution(mesh):
    in_specs = (
        P(None, "dp", "seq", None),
        P(None, "dp", "seq", None),
        P(None, "dp"),
        P(("dp", "seq"), None),
        P(("dp", "seq"), None),
        P(("dp", "seq"), None),
        P(("dp", "seq"), None),
        P(("dp", "seq")),
        P(("dp", "seq")),
        P(("dp", "seq")),
        P(("dp", "seq")),
        P(("dp", "seq")),
        P(("dp", "seq")),
    )
    out_specs = (
        P(None, "dp", "seq", None),
        P(None, "dp", "seq", None),
        P(("dp", "seq"), None),
        P(("dp", "seq"), None),
        P(("dp", "seq"), None),
        P(("dp", "seq"), None),
        P(("dp", "seq")),
        P(("dp", "seq")),
        P(("dp", "seq")),
        P(("dp", "seq")),
        P(("dp", "seq")),
        P(("dp", "seq")),
    )
    return jax.shard_map(
        on_device, mesh=mesh, in_specs=in_specs, out_specs=out_specs, check_vma=False
    )
```

profile of v0, /device:TPU:0, one launch (start us, length us, event | category | flops | bytes accessed | tf_op | source)
XLA Modules:
  0.0 2903.8 jit_solution(11174805176813564353)
XLA Ops:
  8.7 82.5 %all-gather.22.cloned.1.call-done = bf16[2048,2048]{1,0:T(8,128)(2,1)} async-done(((bf16[64,2048]{1,0:T(8,128)(2,1)}), bf16[2048,2048]{1,0:T(8,128)(2,1)}) %all-gather.22.cloned.1.call-update) | async-done | bytes 8388624 | tf_op jit(solution)/shard_map/all_gather | solution.py:313
  106.9 41.3 %all-reduce.19 = (bf16[2048]{0:T(1024)(128)(2,1)S(1)}, bf16[2048]{0:T(1024)(128)(2,1)S(1)}, bf16[6144]{0:T(1024)(128)(2,1)S(1)}, bf16[2048]{0:T(1024)(128)(2,1)}, bf16[2048]{0:T(1024)(128)(2,1)}) all-reduce(bf16[2048]{0:T(1024)(128)(2,1)S(1)} %dynamic-update-slice.1, ...), channel_id=1, replica_groups=mesh['dp'=2,'seq'=16] {'dp','seq'}, use_global_device_ids=true, to_apply=%add.9 | all-reduce | flops 14336 | bytes 57344
  150.6 97.6 %all-gather.16.cloned.1.call-done = bf16[6144,2048]{1,0:T(8,128)(2,1)} async-done(((bf16[192,2048]{1,0:T(8,128)(2,1)}), bf16[6144,2048]{1,0:T(8,128)(2,1)}) %all-gather.16.cloned.1.call-update) | async-done | bytes 25165840 | tf_op jit(solution)/shard_map/all_gather | solution.py:312
  327.5 39.0 %all-gather.2 = bf16[32,1,256]{2,1,0:T(2,128)(2,1)S(1)} all-gather(bf16[1,1,256]{2,1,0:T(2,128)(2,1)S(1)} %reshape.1089), channel_id=1, replica_groups=mesh['dp'=2,'seq'=16] {'dp','seq'}, dimensions={0}, use_global_device_ids=true | all-gather | bytes 16896 | tf_op jit(solution)/shard_map/all_gather | solution.py:320
  416.1 21.1 all_gather.85
  437.4 16.2 all-gather.20.cloned.1.call-done
  468.8 22.4 all_gather.87
  520.5 21.0 all_gather.89
  542.3 16.2 all-gather.30.cloned.1.call-done
  573.6 22.2 all_gather.91
  617.0 44.7 %all-gather.32.cloned.1.call-done = bf16[1,1024,2048]{2,1,0:T(8,128)(2,1)} async-done(((bf16[1,64,2048]{2,1,0:T(8,128)(2,1)}), bf16[1,1024,2048]{2,1,0:T(8,128)(2,1)}) %all-gather.32.cloned.1.call-update) | async-done | bytes 4194320 | tf_op jit(solution)/shard_map/all_gather | solution.py:209
  747.8 25.1 fusion.78
  796.1 61.8 %all-gather.24.cloned.1.call-done = bf16[8192,2048]{1,0:T(8,128)(2,1)} async-done(((bf16[256,2048]{1,0:T(8,128)(2,1)}), bf16[8192,2048]{1,0:T(8,128)(2,1)}) %all-gather.24.cloned.1.call-update) | async-done | bytes 33554448 | tf_op jit(solution)/shard_map/all_gather | solution.py:314
  857.9 17.8 multiply_convert_fusion.9
  875.7 17.3 multiply_convert_fusion.8
  893.1 160.6 %all-gather.26.cloned.1.call-done = bf16[8192,2048]{1,0:T(8,128)(2,1)} async-done(((bf16[256,2048]{1,0:T(8,128)(2,1)}), bf16[8192,2048]{1,0:T(8,128)(2,1)}) %all-gather.26.cloned.1.call-update) | async-done | bytes 33554448 | tf_op jit(solution)/shard_map/all_gather | solution.py:315
  1053.7 16.4 convert_reduce_fusion.3
  1070.1 16.6 convert_reduce_fusion.2
  1086.7 23.1 fusion.70
  1142.1 23.4 fusion.74
  1165.6 132.2 %pad_maximum_fusion = f32[32,768,2048]{2,1,0:T(8,128)} fusion(f32[32,256,2048]{2,1,0:T(8,128)} %bitcast.88, f32[32,256,2048]{2,1,0:T(8,128)} %bitcast.87, f32[32,64,2048]{2,1,0:T(8,128)} %bitcast.301, f32[32,192,2048]{2,1,0:T(8,128)} %bitcast.300), kind=kLoop, calls=%fused_computation | loop fusion | flops 150994944 | bytes 402653184 | tf_op jit(solution)/shard_map/concatenate | solution.py:283
  1299.1 19.9 fusion.219
  1321.7 20.6 fusion.220
  1351.8 1535.2 %reduce-scatter.2.cloned.1.call-done = f32[768,2048]{1,0:T(8,128)} async-done(((f32[24576,2048]{1,0:T(8,128)}), f32[768,2048]{1,0:T(8,128)}) %reduce-scatter.2.cloned.1.call-update) | async-done | bytes 6291472 | tf_op jit(solution)/shard_map/reduce_scatter | solution.py:348
  (369 shorter events, 392.7 us)
Async XLA Ops:
  7.2 84.0 %all-gather.22.cloned.1.call-start = ((), (), s32[]{:S(2)}) async-start(), calls=%async_computation.4 | async-start | bytes 8650752 | tf_op jit(solution)/shard_map/all_gather | solution.py:313
  7.9 240.3 %all-gather.16.cloned.1.call-start = ((), (), s32[]{:S(2)}) async-start(), calls=%async_computation.1 | async-start | bytes 25952256 | tf_op jit(solution)/shard_map/all_gather | solution.py:312
  8.7 370.9 %all-gather.38.cloned.1.call-start = ((), (), s32[]{:S(2)}) async-start(), calls=%async_computation.13 | async-start | bytes 4456448 | tf_op jit(solution)/shard_map/all_gather | solution.py:210
  98.2 287.9 %all-gather.36.cloned.1.call-start = ((), (), s32[]{:S(2)}) async-start(), calls=%async_computation.12 | async-start | bytes 4456448 | tf_op jit(solution)/shard_map/all_gather | solution.py:210
  105.5 296.3 %all-gather.18.cloned.1.call-start = ((), (), s32[]{:S(2)}) async-start(), calls=%async_computation.2 | async-start | bytes 4456448 | tf_op jit(solution)/shard_map/all_gather | solution.py:94
  148.2 100.0 %copy-start.48 = (f32[2048]{0:T(1024)}, f32[2048]{0:T(1024)S(1)}, u32[]{:S(2)}) copy-start(f32[2048]{0:T(1024)S(1)} %convert_element_type.310) | copy-start | bytes 24580
  149.2 99.0 %copy-start.60 = (f32[64]{0:T(128)}, f32[64]{0:T(128)S(1)}, u32[]{:S(2)}) copy-start(f32[64]{0:T(128)S(1)} %get-tuple-element.105) | copy-start | bytes 772
  149.2 99.0 %copy-start.62 = (f32[64]{0:T(128)}, f32[64]{0:T(128)S(1)}, u32[]{:S(2)}) copy-start(f32[64]{0:T(128)S(1)} %get-tuple-element.106) | copy-start | bytes 772
  149.6 98.6 %copy-start.64 = (f32[64]{0:T(128)}, f32[64]{0:T(128)S(1)}, u32[]{:S(2)}) copy-start(f32[64]{0:T(128)S(1)} %fusion.176) | copy-start | bytes 772
  150.2 98.1 %copy-start.66 = (f32[64]{0:T(128)}, f32[64]{0:T(128)S(1)}, u32[]{:S(2)}) copy-start(f32[64]{0:T(128)S(1)} %fusion.177) | copy-start | bytes 772
  150.6 97.7 %copy-start.15 = (bf16[64,2048]{1,0:T(8,128)(2,1)}, bf16[64,2048]{1,0:T(8,128)(2,1)S(1)}, u32[]{:S(2)}) copy-start(bf16[64,2048]{1,0:T(8,128)(2,1)S(1)} %get-tuple-element.71) | copy-start | bytes 786436
  296.6 157.0 %all-gather.20.cloned.1.call-start = ((), (), s32[]{:S(2)}) async-start(), calls=%async_computation.3 | async-start | bytes 4456448 | tf_op jit(solution)/shard_map/all_gather | solution.py:95
  302.4 203.5 %all-gather.28.cloned.1.call-start = ((), (), s32[]{:S(2)}) async-start(), calls=%async_computation.7 | async-start | bytes 4456448 | tf_op jit(solution)/shard_map/all_gather | solution.py:94
  307.3 251.1 %all-gather.30.cloned.1.call-start = ((), (), s32[]{:S(2)}) async-start(), calls=%async_computation.8 | async-start | bytes 4456448 | tf_op jit(solution)/shard_map/all_gather | solution.py:95
  313.1 297.5 %all-gather.34.cloned.1.call-start = ((), (), s32[]{:S(2)}) async-start(), calls=%async_computation.10 | async-start | bytes 4456448 | tf_op jit(solution)/shard_map/all_gather | solution.py:209
  318.1 343.6 %all-gather.32.cloned.1.call-start = ((), (), s32[]{:S(2)}) async-start(), calls=%async_computation.9 | async-start | bytes 4456448 | tf_op jit(solution)/shard_map/all_gather | solution.py:209
  323.5 534.4 %all-gather.24.cloned.1.call-start = ((), (), s32[]{:S(2)}) async-start(), calls=%async_computation.5 | async-start | bytes 34603008 | tf_op jit(solution)/shard_map/all_gather | solution.py:314
  324.2 729.4 %all-gather.26.cloned.1.call-start = ((), (), s32[]{:S(2)}) async-start(), calls=%async_computation.6 | async-start | bytes 34603008 | tf_op jit(solution)/shard_map/all_gather | solution.py:315
  324.8 1021.0 %all-reduce.22.cloned.1.call-start = ((), (), s32[]{:S(2)}) async-start(), calls=%async_computation.14 | async-start | bytes 163840
  875.7 266.3 %copy-start.10 = (bf16[64,8192]{1,0:T(8,128)(2,1)}, bf16[64,8192]{1,0:T(8,128)(2,1)S(1)}, u32[]{:S(2)}) copy-start(bf16[64,8192]{1,0:T(8,128)(2,1)S(1)} %get-tuple-element.94) | copy-start | bytes 3145732
  875.7 177.9 %copy-start.14 = (bf16[2,1,64,2048]{3,2,1,0:T(8,128)(2,1)S(1)}, bf16[2,1,64,2048]{3,2,1,0:T(8,128)(2,1)}, u32[]{:S(2)}) copy-start(bf16[2,1,64,2048]{3,2,1,0:T(8,128)(2,1)} %param.14) | copy-start | bytes 1572868
  893.1 249.0 %copy-start.8 = (bf16[64,8192]{1,0:T(8,128)(2,1)}, bf16[64,8192]{1,0:T(8,128)(2,1)S(1)}, u32[]{:S(2)}) copy-start(bf16[64,8192]{1,0:T(8,128)(2,1)S(1)} %get-tuple-element.88) | copy-start | bytes 3145732
  1165.5 1721.4 %reduce-scatter.2.cloned.1.call-start = ((), (), s32[]{:S(2)}) async-start(), calls=%async_computation.11 | async-start | bytes 207618048 | tf_op jit(solution)/shard_map/reduce_scatter | solution.py:348
  1347.9 1548.4 %copy-start.81 = (f32[64]{0:T(128)}, f32[64]{0:T(128)S(1)}, u32[]{:S(2)}) copy-start(f32[64]{0:T(128)S(1)} %dynamic-slice.3) | copy-start | bytes 772
  (76 other events, 885.9 us)
Sparse Core Ops, SparseCore 0:
  10.9 80.2 all-gather.21
  94.1 154.0 all-gather.15
  250.4 48.9 all-gather.37
  301.4 49.2 all-gather.35
  352.6 49.2 all-gather.17
  403.9 49.6 all-gather.19
  455.8 50.0 all-gather.27
  508.0 50.3 all-gather.29
  560.6 49.9 all-gather.33
  612.6 49.0 all-gather.31
  664.6 193.2 all-gather.23
  860.7 192.9 all-gather.25
  1165.7 120.5 all-reduce.21
  1298.0 1588.9 reduce-scatter.1
where the time goes:
time: 2910 us; the launch traced here: 2900 us
  waiting for transfers between devices  2050 us (70%)
  matrix products  369 us (13%)
  blocking collectives  167 us (6%)
  other arithmetic  165 us (6%)
  local copies, waits for them, and re-layouts  133 us (5%)
    reduce_scatter x1, waiting for transfers between devices, on_device(): lax.psum_scatter(terms_builder(joined_set, row_sizes, model_width, block_...  1540 us
    all_gather x1, waiting for transfers between devices, on_device(): lax.all_gather(fc2_weight, ('dp', 'seq'), axis=0, tiled=True)  161 us
    concatenate x1, other arithmetic, terms_builder(): return jnp.concatenate(term_parts, 1).reshape(row_count, model_width)  132 us
    dot_general x8, matrix products, contract_last(): lax.dot_general(left, right, (((1,), (1,)), ((), ())), preferred_element_...  110 us
    all_gather x1, waiting for transfers between devices, on_device(): lax.all_gather(qkv_weight, ('dp', 'seq'), axis=0, tiled=True)  97.6 us
    all_gather x1, waiting for transfers between devices, on_device(): lax.all_gather(dense_weight, ('dp', 'seq'), axis=0, tiled=True)  82.5 us
    dot_general x4, matrix products, outer_term(): lax.dot_general(left, right, (((0,), (0,)), ((), ())), preferred_element_...  81.2 us
    all_gather x1, waiting for transfers between devices, on_device(): lax.all_gather(fc1_weight, ('dp', 'seq'), axis=0, tiled=True)  61.8 us
  transfers between devices with their start and end apart: 14, of which 11 were waited for; matrix products, arithmetic and copies ran while one was open for 18% of the time, Pallas kernels for 0%

commit v1 on v0

--- a/solution.py
+++ b/solution.py
@@ -4,6 +4,8 @@
 import jax
 import jax.numpy as jnp
 from jax import lax
+from jax.experimental import pallas as pl
+from jax.experimental.pallas import tpu as pltpu
 from jax.sharding import PartitionSpec as P
 
 HEADS = 32
@@ -382,6 +384,453 @@
     )
 
 
+MESH = pl.DeviceIdType.MESH
+BF = jnp.bfloat16
+F32 = jnp.float32
+
+
+def place():
+    d = lax.axis_index("dp")
+    s = lax.axis_index("seq")
+    return d, s, s // 4, (s // 2) % 2, s % 2
+
+
+def seq_of(z, y, c):
+    return z * 4 + y * 2 + c
+
+
+def send(src, dst, ssem, rsem, target):
+    copy = pltpu.make_async_remote_copy(
+        src_ref=src, dst_ref=dst, send_sem=ssem, recv_sem=rsem, device_id=target, device_id_type=MESH
+    )
+    copy.start()
+    return copy
+
+
+def await_bytes(ref, sem):
+    pltpu.make_async_copy(ref, ref, sem).wait()
+
+
+def greet_all():
+    d, s, z, y, c = place()
+    barrier = pltpu.get_barrier_semaphore()
+
+    def greet(k, carry):
+        other = lax.rem(d * 16 + s + k, 32)
+        pl.semaphore_signal(barrier, inc=1, device_id=(other // 16, other % 16), device_id_type=MESH)
+        return carry
+
+    lax.fori_loop(1, 32, greet, 0)
+    pl.semaphore_wait(barrier, 31)
+
+
+class Gather:
+    def __init__(self, src, G, local, zs, zr, ys, yr, cs, cr):
+        self.src, self.G = src, G
+        self.local, self.zs, self.zr, self.ys, self.yr, self.cs, self.cr = local, zs, zr, ys, yr, cs, cr
+        self.sent = []
+
+    def start(self):
+        d, s, z, y, c = place()
+        self.own = pltpu.make_async_copy(self.src, self.G.at[z, y, c], self.local)
+        self.own.start()
+        dst = self.G.at[z, y, c]
+        for dz in (1, 2, 3):
+            self.sent.append(
+                send(self.src, dst, self.zs.at[dz - 1], self.zr.at[dz - 1], (d, seq_of((z + dz) % 4, y, c)))
+            )
+        self.sent.append(send(self.src, dst, self.ys.at[0], self.yr.at[0], (d, seq_of(z, 1 - y, c))))
+
+    def across_y(self):
+        d, s, z, y, c = place()
+        for dz in (1, 2, 3):
+            slot = self.G.at[(z + 4 - dz) % 4, y, c]
+            await_bytes(slot, self.zr.at[dz - 1])
+            self.sent.append(send(slot, slot, self.ys.at[dz], self.yr.at[dz], (d, seq_of(z, 1 - y, c))))
+        self.own.wait()
+        line = self.G.at[:, y, c]
+        self.sent.append(send(line, line, self.cs.at[0], self.cr.at[0], (d, seq_of(z, y, 1 - c))))
+
+    def across_core(self):
+        d, s, z, y, c = place()
+        for dz in (0, 1, 2, 3):
+            await_bytes(self.G.at[(z + 4 - dz) % 4, 1 - y, c], self.yr.at[dz])
+        line = self.G.at[:, 1 - y, c]
+        self.sent.append(send(line, line, self.cs.at[1], self.cr.at[1], (d, seq_of(z, y, 1 - c))))
+
+    def finish(self):
+        d, s, z, y, c = place()
+        await_bytes(self.G.at[:, y, 1 - c], self.cr.at[0])
+        await_bytes(self.G.at[:, 1 - y, 1 - c], self.cr.at[1])
+        for copy in self.sent:
+            copy.wait_send()
+
+
+class Scatter:
+    def __init__(self, P, RC, RY, RZ, cs, cr, ys, yr, zs, zr):
+        self.P, self.RC, self.RY, self.RZ = P, RC, RY, RZ
+        self.cs, self.cr, self.ys, self.yr, self.zs, self.zr = cs, cr, ys, yr, zs, zr
+        self.sent = []
+
+    def start(self):
+        d, s, z, y, c = place()
+        for k, row in ((0, 1 - y), (1, y)):
+            self.sent.append(
+                send(
+                    self.P.at[:, row, 1 - c], self.RC.at[:, row], self.cs.at[k], self.cr.at[k], (d, seq_of(z, y, 1 - c))
+                )
+            )
+
+    def across_y(self):
+        d, s, z, y, c = place()
+        await_bytes(self.RC.at[:, 1 - y], self.cr.at[0])
+        for dz in (1, 2, 3, 0):
+            zz = (z + dz) % 4
+            chunk = self.P.at[zz, 1 - y, c]
+            chunk[...] = (chunk[...].astype(F32) + self.RC[zz, 1 - y].astype(F32)).astype(BF)
+            self.sent.append(
+                send(chunk, self.RY.at[zz], self.ys.at[dz], self.yr.at[dz], (d, seq_of(z, 1 - y, c)))
+            )
+
+    def across_z(self):
+        d, s, z, y, c = place()
+        await_bytes(self.RC.at[:, y], self.cr.at[1])
+        for dz in (1, 2, 3):
+            zz = (z + dz) % 4
+            await_bytes(self.RY.at[zz], self.yr.at[dz])
+            chunk = self.P.at[zz, y, c]
+            chunk[...] = (
+                chunk[...].astype(F32) + self.RC[zz, y].astype(F32) + self.RY[zz].astype(F32)
+            ).astype(BF)
+            self.sent.append(
+                send(chunk, self.RZ.at[dz - 1], self.zs.at[dz - 1], self.zr.at[dz - 1], (d, seq_of(zz, y, c)))
+            )
+
+    def finish(self):
+        d, s, z, y, c = place()
+        await_bytes(self.RY.at[z], self.yr.at[0])
+        total = self.P[z, y, c].astype(F32) + self.RC[z, y].astype(F32) + self.RY[z].astype(F32)
+        for k in (0, 1, 2):
+            await_bytes(self.RZ.at[k], self.zr.at[k])
+            total = total + self.RZ[k].astype(F32)
+        for copy in self.sent:
+            copy.wait_send()
+        return total
+
+
+def gather_kernel(
+    x_ref, dy_ref, wq_ref, wd_ref, w1_ref, w2_ref,
+    N, DY, Wq, Wd, W1, W2,
+    local, zs, zr, ys, yr, cs, cr, qs, qr, qxs, qxr, ws, wr, wl,
+):
+    d, s, z, y, c = place()
+    greet_all()
+    jobs = []
+    for t, (src, G) in enumerate(((x_ref, N), (dy_ref, DY))):
+        for m in range(2):
+            jobs.append(
+                Gather(src.at[m], G.at[m], local.at[t, m], zs.at[t, m], zr.at[t, m], ys.at[t, m], yr.at[t, m], cs.at[t, m], cr.at[t, m])
+            )
+    jobs[0].start()
+    me = d * 16 + s
+    for i in range(3):
+        b = me * 3 + i
+        target, entry = b % 16, b // 16
+
+        @pl.when(target == s)
+        def _():
+            pltpu.make_async_copy(wq_ref.at[i], Wq.at[entry], qr.at[entry]).start()
+
+        @pl.when(target != s)
+        def _():
+            send(wq_ref.at[i], Wq.at[entry], qs.at[i], qr.at[entry], (d, target))
+
+    partner = (1 - d, s)
+    moved = []
+    for k, (src, dst) in enumerate(((w1_ref, W1), (w2_ref, W2), (wd_ref, Wd))):
+        own = pltpu.make_async_copy(src, dst.at[d], wl.at[k])
+        own.start()
+        moved.append((own, send(src, dst.at[d], ws.at[k], wr.at[k], partner)))
+    jobs[1].start()
+    jobs[2].start()
+    jobs[3].start()
+    for i in range(3):
+        entry = 3 * d + i
+        await_bytes(Wq.at[entry], qr.at[entry])
+    mine = Wq.at[pl.ds(3 * d, 3)]
+    qx = send(mine, mine, qxs.at[0], qxr.at[0], partner)
+    for job in jobs:
+        job.across_y()
+    for job in jobs:
+        job.across_core()
+    for job in jobs:
+        job.finish()
+    for k, (own, copy) in enumerate(moved):
+        own.wait()
+        copy.wait()
+    qx.wait()
+    for i in range(3):
+        target = (me * 3 + i) % 16
+
+        @pl.when(target != s)
+        def _():
+            await_bytes(wq_ref.at[i], qs.at[i])
+
+
+def run_gather(x, dy, wq, wd, w1, w2):
+    width = x.shape[-1]
+    anyspace = pl.BlockSpec(memory_space=pl.ANY)
+    dma = pltpu.SemaphoreType.DMA
+    return pl.pallas_call(
+        gather_kernel,
+        name="gather_all",
+        out_shape=(
+            jax.ShapeDtypeStruct((2, 4, 2, 2, 64, width), BF),
+            jax.ShapeDtypeStruct((2, 4, 2, 2, 64, width), BF),
+            jax.ShapeDtypeStruct((6, 64, width), BF),
+            jax.ShapeDtypeStruct((2, 64, width), BF),
+            jax.ShapeDtypeStruct((2, 256, width), BF),
+            jax.ShapeDtypeStruct((2, 256, width), BF),
+        ),
+        in_specs=[anyspace] * 6,
+        out_specs=(anyspace,) * 6,
+        scratch_shapes=[
+            dma((2, 2)), dma((2, 2, 3)), dma((2, 2, 3)), dma((2, 2, 4)), dma((2, 2, 4)), dma((2, 2, 2)), dma((2, 2, 2)),
+            dma((3,)), dma((6,)), dma((1,)), dma((1,)), dma((3,)), dma((3,)), dma((3,)),
+        ],
+        compiler_params=pltpu.CompilerParams(collective_id=0, has_side_effects=True),
+    )(x, dy, wq.reshape(3, 64, width), wd, w1, w2)
+
+
+def scatter_kernel(
+    po_ref, pg_ref, gq_ref, gx_ref, O, GN, RX, RQ,
+    P, RC, RY, RZ, SQ, XB, load, cs, cr, ys, yr, zs, zr, xs, xr, qs, qr,
+):
+    d, s, z, y, c = place()
+    loads = []
+    for t, src in enumerate((po_ref, pg_ref)):
+        for m in range(2):
+            copy = pltpu.make_async_copy(src.at[m], P.at[t, m], load.at[t, m])
+            copy.start()
+            loads.append(copy)
+    greet_all()
+    partner = (1 - d, s)
+    xq = send(gq_ref.at[pl.ds(3 * (1 - d), 3)], XB, xs.at[0], xr.at[0], partner)
+    xo = send(gx_ref, RX, xs.at[1], xr.at[1], partner)
+    jobs = []
+    for t in range(2):
+        for m in range(2):
+            jobs.append(
+                Scatter(P.at[t, m], RC.at[t, m], RY.at[t, m], RZ.at[t, m],
+                        cs.at[t, m], cr.at[t, m], ys.at[t, m], yr.at[t, m], zs.at[t, m], zr.at[t, m])
+            )
+    for load_copy, job in zip(loads, jobs):
+        load_copy.wait()
+        job.start()
+    for job in jobs:
+        job.across_y()
+    for job in jobs:
+        job.across_z()
+    xq.wait_recv()
+    keep = pltpu.make_async_copy(gq_ref.at[pl.ds(3 * d, 3)], SQ, load.at[0, 0])
+    keep.start()
+    keep.wait()
+    for i in range(3):
+        SQ[i] = (SQ[i].astype(F32) + XB[i].astype(F32)).astype(BF)
+        b = s + 16 * (3 * d + i)
+        owner = b // 3 - 16 * d
+        where = b % 3
+
+        @pl.when(owner == s)
+        def _():
+            pltpu.make_async_copy(SQ.at[i], RQ.at[where], qr.at[where]).start()
+
+        @pl.when(owner != s)
+        def _():
+            send(SQ.at[i], RQ.at[where], qs.at[i], qr.at[where], (d, owner))
+
+    for k, job in enumerate(jobs):
+        total = job.finish()
+        if k < 2:
+            O[k] = total
+        else:
+            GN[k - 2] = total
+    for i in range(3):
+        await_bytes(RQ.at[i], qr.at[i])
+        b = s + 16 * (3 * d + i)
+        owner = b // 3 - 16 * d
+
+        @pl.when(owner != s)
+        def _():
+            await_bytes(SQ.at[i], qs.at[i])
+
+    xq.wait_send()
+    xo.wait()
+
+
+def run_scatter(po, pg, gq, gx):
+    width = po.shape[-1]
+    vm = pl.BlockSpec(memory_space=pltpu.VMEM)
+    anyspace = pl.BlockSpec(memory_space=pl.ANY)
+    dma = pltpu.SemaphoreType.DMA
+    return pl.pallas_call(
+        scatter_kernel,
+        name="scatter_all",
+        out_shape=(
+            jax.ShapeDtypeStruct((2, 64, width), F32),
+            jax.ShapeDtypeStruct((2, 64, width), F32),
+            jax.ShapeDtypeStruct(gx.shape, BF),
+            jax.ShapeDtypeStruct((3, 64, width), BF),
+        ),
+        in_specs=[anyspace] * 4,
+        out_specs=(vm, vm, anyspace, anyspace),
+        scratch_shapes=[
+            pltpu.VMEM((2, 2, 4, 2, 2, 64, width), BF),
+            pltpu.VMEM((2, 2, 4, 2, 64, width), BF),
+            pltpu.VMEM((2, 2, 4, 64, width), BF),
+            pltpu.VMEM((2, 2, 3, 64, width), BF),
+            pltpu.VMEM((3, 64, width), BF),
+            pltpu.VMEM((3, 64, width), BF),
+            dma((2, 2)), dma((2, 2, 2)), dma((2, 2, 2)), dma((2, 2, 4)), dma((2, 2, 4)), dma((2, 2, 3)), dma((2, 2, 3)),
+            dma((2,)), dma((2,)), dma((3,)), dma((3,)),
+        ],
+        compiler_params=pltpu.CompilerParams(
+            collective_id=1, has_side_effects=True, vmem_limit_bytes=60 * 2**20
+        ),
+    )(po, pg, gq, gx)
+
+
+def outer(left, right):
+    return lax.dot_general(left, right, (((0,), (0,)), ((), ())), preferred_element_type=F32)
+
+
+def by_heads(
+    hidden_in, cotangent, prefix_len, qkv_weight, dense_weight, fc1_weight, fc2_weight,
+    norm_gain, norm_shift, qkv_bias, dense_bias, fc1_bias, fc2_bias,
+):
+    width = hidden_in.shape[-1]
+    length = hidden_in.shape[2] * 16
+    d, s, z, y, c = place()
+    small = jnp.concatenate([norm_gain, norm_shift, dense_bias, fc2_bias, qkv_bias, fc1_bias])
+    small = lax.all_gather(small, ("dp", "seq"), axis=0).astype(F32)
+    gain, shift, dense_add, fc2_add = (small[:, 64 * i : 64 * i + 64].reshape(-1) for i in range(4))
+    qkv_blocks = small[:, 256:448].reshape(96, 64)
+    qkv_add = jnp.take(qkv_blocks, s + 16 * jnp.arange(6), axis=0).reshape(3, 128)
+    fc1_blocks = small[:, 448:704]
+    fc1_add = jnp.take(fc1_blocks, s + 16 * jnp.arange(2), axis=0).reshape(512)
+
+    rows = hidden_in.reshape(128, width).astype(F32)
+    centred = rows - jnp.mean(rows, 1, keepdims=True)
+    rstd = lax.rsqrt(jnp.mean(centred * centred, 1, keepdims=True) + NORM_EPS)
+    xhat = centred * rstd
+    normed = (xhat * gain + shift).astype(BF)
+
+    N, DY, Wq, Wd, W1, W2 = run_gather(
+        normed.reshape(2, 64, width), cotangent.reshape(2, 64, width), qkv_weight, dense_weight, fc1_weight, fc2_weight
+    )
+    Nf = N.reshape(2, length, width)
+    DYf = DY.reshape(2, length, width)
+    Wq = Wq.reshape(384, width)
+    Wd = Wd.reshape(128, width)
+    W1 = W1.reshape(512, width)
+    W2 = W2.reshape(512, width)
+    cosine, sine = rotary_tables(0, length)
+    scale = 1.0 / math.sqrt(HEAD)
+    po, pg, gms, ghs, acts, mixes = [], [], [], [], [], []
+    for m in range(2):
+        merged = (contract_last(Nf[m], Wq) + qkv_add.reshape(384)).reshape(length, 3, 2, HEAD)
+        query = rotate(merged[:, 0], cosine, sine).astype(BF)
+        key = rotate(merged[:, 1], cosine, sine).astype(BF)
+        value = merged[:, 2].astype(BF)
+        scores = jnp.einsum("qhd,khd->hqk", query, key, preferred_element_type=F32) * scale
+        places = jnp.arange(length, dtype=jnp.int32)
+        visible = (places[None, :] <= jnp.maximum(places[:, None], prefix_len[m, 0] - 1))[None]
+        masked = jnp.where(visible, scores, MASKED_LOW)
+        top = jnp.max(masked, -1, keepdims=True)
+        weights = jnp.where(visible, jnp.exp(masked - top), 0.0)
+        total = jnp.sum(weights, -1, keepdims=True)
+        mixed = jnp.einsum("hqk,khd->hqd", weights.astype(BF), value, preferred_element_type=F32) / total
+        probs = weights / total
+        mixed_low = mixed.transpose(1, 0, 2).reshape(length, 128).astype(BF)
+        pre = contract_last(Nf[m], W1) + fc1_add
+        act = gelu_tanh(pre).astype(BF)
+        po.append(
+            (
+                jnp.dot(mixed_low, Wd, preferred_element_type=F32) + jnp.dot(act, W2, preferred_element_type=F32)
+            ).astype(BF)
+        )
+        grad_mixed = contract_last(DYf[m], Wd).astype(BF)
+        grad_act = contract_last(DYf[m], W2)
+        grad_hidden = jax.vjp(gelu_tanh, pre)[1](grad_act)[0].astype(BF)
+        gm_heads = grad_mixed.reshape(length, 2, HEAD)
+        delta = jnp.sum(gm_heads.astype(F32).transpose(1, 0, 2) * mixed, -1, keepdims=True)
+        grad_probs = jnp.einsum("qhd,khd->hqk", gm_heads, value, preferred_element_type=F32)
+        grad_scores = (probs * (grad_probs - delta)).astype(BF)
+        grad_query = scale * jnp.einsum("hqk,khd->qhd", grad_scores, key, preferred_element_type=F32)
+        grad_key = scale * jnp.einsum("hqk,qhd->khd", grad_scores, query, preferred_element_type=F32)
+        grad_value = jnp.einsum("hqk,qhd->khd", probs.astype(BF), gm_heads, preferred_element_type=F32)
+        pull = jax.vjp(partial(rotate, cosine=cosine, sine=sine), grad_query)[1]
+        grad_merged = jnp.stack([pull(grad_query)[0], pull(grad_key)[0], grad_value], 1)
+        grad_merged = grad_merged.reshape(length, 384).astype(BF)
+        pg.append(
+            (
+                jnp.dot(grad_merged, Wq, preferred_element_type=F32)
+                + jnp.dot(grad_hidden, W1, preferred_element_type=F32)
+            ).astype(BF)
+        )
+        gms.append(grad_merged)
+        ghs.append(grad_hidden)
+        acts.append(act)
+        mixes.append(mixed_low)
+    Nall, DYall = Nf.reshape(2 * length, width), DYf.reshape(2 * length, width)
+    gm, gh, act, mixed_low = (jnp.concatenate(p, 0) for p in (gms, ghs, acts, mixes))
+    gq = outer(gm, Nall)
+    gd = outer(mixed_low, DYall).reshape(2, 64, width)
+    g1 = outer(gh, Nall).reshape(2, 256, width)
+    g2 = outer(act, DYall).reshape(2, 256, width)
+
+    def pick(pair, which):
+        return lax.dynamic_index_in_dim(pair, which, 0, False)
+
+    gx = jnp.concatenate([pick(gd, 1 - d), pick(g1, 1 - d), pick(g2, 1 - d)], 0).astype(BF)
+    chunks = (2, 4, 2, 2, 64, width)
+    O, GN, RX, RQ = run_scatter(
+        jnp.stack(po).reshape(chunks), jnp.stack(pg).reshape(chunks), gq.astype(BF).reshape(6, 64, width), gx
+    )
+    RX = RX.astype(F32)
+    hidden_out = (rows.reshape(2, 64, width) + O + (dense_add + fc2_add)).astype(BF)
+    dense_grad = pick(gd, d) + RX[:64]
+    fc1_grad = pick(g1, d) + RX[64:320]
+    fc2_grad = pick(g2, d) + RX[320:]
+    qkv_grad = RQ.astype(F32).reshape(192, width)
+    grad_normed = GN.reshape(128, width)
+    g = grad_normed * gain
+    input_grad = cotangent.reshape(128, width).astype(F32) + rstd * (
+        g - jnp.mean(g, 1, keepdims=True) - xhat * jnp.mean(g * xhat, 1, keepdims=True)
+    )
+    gain_sum = jnp.sum(grad_normed * xhat, 0).reshape(32, 64)
+    shift_sum = jnp.sum(grad_normed, 0).reshape(32, 64)
+    dy_sum = jnp.sum(cotangent.reshape(128, width).astype(F32), 0).reshape(32, 64)
+    qb = jnp.zeros((96, 64), F32).at[s + 16 * jnp.arange(6)].set(jnp.sum(gm.astype(F32), 0).reshape(6, 64))
+    fb = jnp.zeros((32, 256), F32).at[s + 16 * jnp.arange(2)].set(jnp.sum(gh.astype(F32), 0).reshape(2, 256))
+    packed = jnp.concatenate([gain_sum, shift_sum, dy_sum, qb.reshape(32, 192), fb], 1)
+    packed = lax.psum_scatter(packed, ("dp", "seq"), scatter_dimension=0, tiled=True)[0]
+    return (
+        hidden_out.reshape(hidden_in.shape),
+        input_grad.reshape(hidden_in.shape),
+        qkv_grad,
+        dense_grad,
+        fc1_grad,
+        fc2_grad,
+        packed[:64],
+        packed[64:128],
+        packed[192:384],
+        packed[128:192],
+        packed[384:640],
+        packed[128:192],
+    )
+
+
 def solution(mesh):
     in_specs = (
         P(None, "dp", "seq", None),
@@ -412,6 +861,11 @@
         P(("dp", "seq")),
         P(("dp", "seq")),
     )
+    fits = mesh.shape["dp"] == 2 and mesh.shape["seq"] == 16
+
+    def body(*args):
+        return (by_heads if fits and args[0].shape[0] == 2 and args[0].shape[2] == 64 else on_device)(*args)
+
     return jax.shard_map(
-        on_device, mesh=mesh, in_specs=in_specs, out_specs=out_specs, check_vma=False
-    )
+        body, mesh=mesh, in_specs=in_specs, out_specs=out_specs, check_vma=False
+    )

time: 2910 us -> 668 us (0.23)
  waiting for transfers between devices: 2050 us -> 116 us
  Pallas kernels: 0 us -> 251 us
  matrix products: 369 us -> 140 us
  blocking collectives: 167 us -> 42.5 us
  other arithmetic: 165 us -> 47.3 us
  local copies, waits for them, and re-layouts: 133 us -> 44.2 us
    reduce_scatter x1 -> x0, waiting for transfers between devices: 1540 us -> none  [on_device(): lax.psum_scatter(terms_builder(joined_set, row_sizes, model_width, block_...]
    all_gather x12 -> x0, waiting for transfers between devices: 514 us -> none  [the longest x1 161 us: on_device(): lax.all_gather(fc2_weight, ('dp', 'seq'), axis=0, tiled=True)]
    pallas_call x0 -> x2, Pallas kernels: none -> 251 us  [the longest x1 141 us: run_gather(): pl.pallas_call(gather_kernel, name='gather_all', out_shape=(jax.ShapeDtyp...]
    dot_general x24 -> x22, matrix products: 260 us -> 93.9 us  [the longest x4 29.7 us: outer(): lax.dot_general(left, right, (((0,), (0,)), ((), ())), preferred_element_...]
    concatenate x5 -> x2, other arithmetic: 137 us -> 1.67 us  [the longest x1 1.63 us: by_heads(): jnp.concatenate([pick(gd, 1 - d), pick(g1, 1 - d), pick(g2, 1 - d)], 0)]
    all_gather x5 -> x0, blocking collectives: 126 us -> none  [the longest x2 44.6 us: backward_part(): lax.all_gather(delta.transpose(0, 2, 1), 'seq', axis=1, tiled=True)]
    unnamed x15 -> x2, waiting for transfers between devices: 2.75 us -> 116 us
    dot_general x8, matrix products: 110 us -> 31 us  [contract_last(): lax.dot_general(left, right, (((1,), (1,)), ((), ())), preferred_element_...]
  transfers between devices with their start and end apart: 14 -> 1, of which waited for: 11 -> 1; matrix products, arithmetic and copies ran while one was open for 18% -> 2% of each run, Pallas kernels for 0% -> 0%
where the time goes in v1:
time: 668 us; the launch traced here: 658 us
  Pallas kernels  251 us (38%)
  matrix products  140 us (21%)
  waiting for transfers between devices  116 us (17%)
  other arithmetic  47.3 us (7%)
  local copies, waits for them, and re-layouts  44.2 us (7%)
  blocking collectives  42.5 us (6%)
  between operations  16.8 us (3%)
    pallas_call x1, Pallas kernels, run_gather(): pl.pallas_call(gather_kernel, name='gather_all', out_shape=(jax.ShapeDtyp...  141 us
    unnamed x2, waiting for transfers between devices  116 us
    pallas_call x1, Pallas kernels, run_scatter(): pl.pallas_call(scatter_kernel, name='scatter_all', out_shape=(jax.ShapeDt...  110 us
    unnamed x1, blocking collectives  42.5 us
    dot_general x8, matrix products, contract_last(): lax.dot_general(left, right, (((1,), (1,)), ((), ())), preferred_element_...  31 us
    dot_general x4, matrix products, outer(): lax.dot_general(left, right, (((0,), (0,)), ((), ())), preferred_element_...  29.7 us
    sub x2, matrix products, by_heads(): weights = jnp.where(visible, jnp.exp(masked - top), 0.0)  15.4 us
  transfers between devices with their start and end apart: 1, of which 1 were waited for; matrix products, arithmetic and copies ran while one was open for 2% of the time, Pallas kernels for 0%

profile of v1, /device:TPU:0, one launch (start us, length us, event | category | flops | bytes accessed | tf_op | source)
XLA Modules:
  0.0 657.7 jit_solution(11113671403662035260)
XLA Ops:
  11.6 42.5 %all-reduce.16 = bf16[22528]{0:T(1024)(128)(2,1)S(1)} all-reduce(bf16[22528]{0:T(1024)(128)(2,1)S(1)} %dynamic-update-slice), channel_id=2, replica_groups=mesh['dp'=2,'seq'=16] {'dp','seq'}, use_global_device_ids=true, to_apply=%add.16 | all-reduce | flops 22528 | bytes 90112
  60.6 140.8 %gather_all.1 = (bf16[2,4,2,2,64,2048]{5,4,3,2,1,0:T(8,128)(2,1)}, bf16[2,4,2,2,64,2048]{5,4,3,2,1,0:T(8,128)(2,1)}, bf16[6,64,2048]{2,1,0:T(8,128)(2,1)}, bf16[...) custom-call(bf16[2,64,2048]{2,1,0:T(8,128)(2,1)} %fusion.57.x_ref, ...), custom_call_target="tpu_custom_call" | custom-call | tf_op jit(solution)/shard_map/gather_all/pallas_call | solution.py:584
  201.3 9.5 %fusion.115 = (bf16[1,4,2,2,64,2048]{5,4,3,2,1,0:T(8,128)(2,1)}, bf16[1,4,2,2,64,2048]{5,4,3,2,1,0:T(8,128)(2,1)}, bf16[1,4,2,2,64,2048]{5,4,3,2,1,0:T(8,128)(2,1)S(1)}, bf16[1,4,2,2,64,2048]{5,4,3,2,1,0:T(8,128)(2,1)S(1)}) fusion(bf16[2,4,2,2,64,2048]{5,4,3,2,1,0:T(8,128)(2,1)} %get-tuple-element.27, bf16[2,4,2,2,64,2048]{5,4,3,2,1,0:T(8,128)(2,1)} %get-tuple-element.22), kind=kLoop, calls=%fused_computation.232 | loop fusion | bytes 33554432 | tf_op jit(solution)/shard_map/slice | solution.py:762
  219.8 7.8 %fusion.126 = (f32[2,1024]{1,0:T(2,128)S(1)}, f32[2,1024,1024]{1,2,0:T(8,128)}) fusion(pred[1024,1024]{0,1:T(8,128)(4,1)} %iota_compare_fusion, bf16[1024,2,32]{0,2,1:T(8,128)(2,1)S(1)} %slice.293, bf16[1024,2,32]{0,2,1:T(8,128)(2,1)S(1)} %get-tuple-element.116, bf16[1024,2,32]{0,2,1:T(8,128)(2,1)S(1)} %slice.294, ...), kind=kOutput, calls=%fused_computation.243 | convolution fusion | flops 279970816 | bytes 9969664 | tf_op jit(solution)/shard_map/sub | solution.py:750
  227.7 4.6 fusion.71
  232.2 4.3 convolution_convert_fusion.1
  247.6 7.6 %fusion.127 = (f32[2,1024]{1,0:T(2,128)S(1)}, f32[2,1024,1024]{1,2,0:T(8,128)}) fusion(pred[1024,1024]{0,1:T(8,128)(4,1)} %iota_compare_fusion.1, bf16[1024,2,32]{0,2,1:T(8,128)(2,1)S(1)} %slice.295, bf16[1024,2,32]{0,2,1:T(8,128)(2,1)S(1)} %get-tuple-element.114, bf16[1024,2,32]{0,2,1:T(8,128)(2,1)S(1)} %copy-done.36, ...), kind=kOutput, calls=%fused_computation.244 | convolution fusion | flops 279970816 | bytes 9969664 | tf_op jit(solution)/shard_map/sub | solution.py:750
  255.2 5.1 fusion.72
  283.9 9.8 %fusion.23 = (bf16[1024,512]{1,0:T(8,128)(2,1)S(1)}, bf16[1024,512]{1,0:T(8,128)(2,1)S(1)}, bf16[1024,512]{1,0:T(8,128)(2,1)S(1)}, bf16[1024,512]{1,0:T(8,128)(2,1)S(1)}) fusion(f32[1024,512]{1,0:T(8,128)} %fusion.128, f32[512]{0:T(512)S(1)} %bitcast.296, f32[1024,512]{1,0:T(8,128)} %fusion.130, f32[1024,512]{1,0:T(8,128)} %fusion.133, ...), kind=kOutput, calls=%fused_computation.55 | convolution fusion | flops 2175795200 | bytes 16779264 | tf_op jit(solution)/shard_map/dot_general | solution.py:56
  293.7 5.6 fusion.132
  300.8 5.6 fusion.134
  306.4 5.6 fusion.129
  312.2 5.7 fusion.131
  326.8 5.6 fusion.135
  334.2 7.6 %fusion.136 = f32[2,256,2048]{2,1,0:T(8,128)S(1)} fusion(bf16[2,256,2048]{2,1,0:T(8,128)(2,1)} %bitcast.277, bf16[2048,2048,1]{1,0,2:T(8,128)(2,1)} %bitcast.252), kind=kOutput, calls=%fused_computation.253 | convolution fusion | flops 4294967296 | bytes 14680064 | tf_op jit(solution)/shard_map/dot_general | solution.py:704
  347.3 7.6 %fusion.137 = f32[2,256,2048]{2,1,0:T(8,128)S(1)} fusion(bf16[2,256,2048]{2,1,0:T(8,128)(2,1)} %bitcast.278, bf16[2048,2048,1]{1,0,2:T(8,128)(2,1)} %bitcast.235), kind=kOutput, calls=%fused_computation.254 | convolution fusion | flops 4294967296 | bytes 14680064 | tf_op jit(solution)/shard_map/dot_general | solution.py:704
  357.6 8.9 %convolution_convert_fusion = bf16[384,2048]{1,0:T(8,128)(2,1)} fusion(bf16[2048,2048]{1,0:T(8,128)(2,1)} %bitcast.253, bf16[1024,384]{0,1:T(8,128)(2,1)S(1)} %bitcast.258, bf16[1024,384]{0,1:T(8,128)(2,1)S(1)} %bitcast.255), kind=kOutput, calls=%fused_computation.50 | convolution fusion | flops 3225157632 | bytes 11534336 | tf_op jit(solution)/shard_map/dot_general | solution.py:704
  366.6 4.6 add_convert_fusion.1
  371.3 6.1 add_convert_fusion
  384.1 7.7 %pad_maximum_fusion.1.pg_ref = bf16[2,4,2,2,64,2048]{5,4,3,2,1,0:T(8,128)(2,1)} fusion(bf16[1,4,2,2,64,2048]{5,4,3,2,1,0:T(8,128)(2,1)} %bitcast.237, bf16[1,4,2,2,64,2048]{5,4,3,2,1,0:T(8,128)(2,1)} %bitcast.236), kind=kLoop, calls=%fused_computation.7 | loop fusion | flops 4194304 | bytes 16777216 | tf_op jit(solution)/shard_map/stack | solution.py:798
  391.8 6.4 pad_maximum_fusion.po_ref
  399.9 109.8 %scatter_all.1 = (f32[2,64,2048]{2,1,0:T(8,128)}, f32[2,64,2048]{2,1,0:T(8,128)}, bf16[576,2048]{1,0:T(8,128)(2,1)}, bf16[3,64,2048]{2,1,0:T(8,128)(2,1)}) custom-call(bf16[2,4,2,2,64,2048]{5,4,3,2,1,0:T(8,128)(2,1)} %pad_maximum_fusion.po_ref, bf16[2,4,2,2,64,2048]{5,4,3,2,1,0:T(8,128)(2,1)} %pad_maximum_fusion.1.pg_ref, bf16[6,64,2048]{2,1,0:T(8,128)(2,1)} %bitcast.280, ...), custom_call_target="tpu_custom_call" | custom-call | tf_op jit(solution)/shard_map/scatter_all/pallas_call | solution.py:676
  521.3 6.6 %slice_add_fusion = (f32[256,2048]{1,0:T(8,128)}, f32[256,2048]{1,0:T(8,128)}) fusion(f32[576,2048]{1,0:T(8,128)} %convert_element_type.201, f32[2,256,2048]{2,1,0:T(8,128)} %copy-done.19, s32[]{:T(128)S(6)} %select_n.94, f32[2,256,2048]{2,1,0:T(8,128)} %copy-done.18), kind=kLoop, calls=%fused_computation.64 | loop fusion | flops 1048576 | bytes 12582916 | tf_op jit(solution)/shard_map/add | solution.py:804
  529.9 116.0 %all-reduce.20.cloned.1.call-done = f32[32,640]{1,0:T(8,128)} async-done(((f32[32,640]{1,0:T(8,128)}), f32[32,640]{1,0:T(8,128)}) %all-reduce.20.cloned.1.call-update) | async-done | bytes 81936
  (258 shorter events, 99.6 us)
Async XLA Ops:
  7.2 638.7 %all-reduce.20.cloned.1.call-start = ((), (), s32[]{:S(2)}) async-start(), calls=%async_computation | async-start | bytes 163840
  54.9 155.9 %copy-start.43 = (f32[2048]{0:T(1024)}, f32[2048]{0:T(1024)S(1)}, u32[]{:S(2)}) copy-start(f32[2048]{0:T(1024)S(1)} %mul.378) | copy-start | bytes 24580
  56.2 154.6 %copy-start.47 = (f32[2,64]{1,0:T(2,128)}, f32[2,64]{1,0:T(2,128)S(1)}, u32[]{:S(2)}) copy-start(f32[2,64]{1,0:T(2,128)S(1)} %broadcast_multiply_fusion.3) | copy-start | bytes 1540
  57.6 153.3 %copy-start.49 = (f32[2,64]{1,0:T(2,128)}, f32[2,64]{1,0:T(2,128)S(1)}, u32[]{:S(2)}) copy-start(f32[2,64]{1,0:T(2,128)S(1)} %add_rsqrt_fusion) | copy-start | bytes 1540
  201.3 9.6 %copy-start.5 = (bf16[6,64,2048]{2,1,0:T(8,128)(2,1)S(1)}, bf16[6,64,2048]{2,1,0:T(8,128)(2,1)}, u32[]{:S(2)}) copy-start(bf16[6,64,2048]{2,1,0:T(8,128)(2,1)} %get-tuple-element.23) | copy-start | bytes 4718596
  216.5 11.1 %copy-start.28 = (f32[1024,32]{0,1:T(8,128)}, f32[1024,32]{0,1:T(8,128)S(1)}, u32[]{:S(2)}) copy-start(f32[1024,32]{0,1:T(8,128)S(1)} %get-tuple-element.127) | copy-start | bytes 393220
  219.8 7.8 %copy-start.32 = (bf16[1024,2,32]{0,2,1:T(8,128)(2,1)}, bf16[1024,2,32]{0,2,1:T(8,128)(2,1)S(1)}, u32[]{:S(2)}) copy-start(bf16[1024,2,32]{0,2,1:T(8,128)(2,1)S(1)} %get-tuple-element.116) | copy-start | bytes 393220
  227.6 9.0 %slice-start.8 = ((s8[8388608]{0:T(1024)(128)(4,1)}), s8[4194304]{0:T(1024)(128)(4,1)S(1)}, s32[]{:S(2)}) async-start(s8[8388608]{0:T(1024)(128)(4,1)} %bitcast.248), calls=%async_computation.9 | async-start | bytes 8388608
  227.6 9.0 %slice-start.9 = ((s8[8388608]{0:T(1024)(128)(4,1)}), s8[4194304]{0:T(1024)(128)(4,1)S(1)}, s32[]{:S(2)}) async-start(s8[8388608]{0:T(1024)(128)(4,1)} %bitcast.248), calls=%async_computation.10 | async-start | bytes 8388608
  283.9 9.8 %copy-start.56 = (bf16[2,256,2048]{2,1,0:T(8,128)(2,1)S(1)}, bf16[2,256,2048]{2,1,0:T(8,128)(2,1)}, u32[]{:S(2)}) copy-start(bf16[2,256,2048]{2,1,0:T(8,128)(2,1)} %get-tuple-element.25) | copy-start | bytes 6291460
  347.3 10.3 %copy-start.4 = (bf16[1024,3,2,64]{0,3,2,1:T(8,128)(2,1)S(1)}, bf16[1024,3,2,64]{0,3,2,1:T(8,128)(2,1)}, u32[]{:S(2)}) copy-start(bf16[1024,3,2,64]{0,3,2,1:T(8,128)(2,1)} %copy-done.3) | copy-start | bytes 2359300
  355.0 11.6 %slice-start.2 = ((s8[8388608]{0:T(1024)(128)(4,1)}), s8[4194304]{0:T(1024)(128)(4,1)S(1)}, s32[]{:S(2)}) async-start(s8[8388608]{0:T(1024)(128)(4,1)} %bitcast.242), calls=%async_computation.3 | async-start | bytes 8388608
  355.0 16.2 %slice-start = ((s8[8388608]{0:T(1024)(128)(4,1)}), s8[4194304]{0:T(1024)(128)(4,1)S(1)}, s32[]{:S(2)}) async-start(s8[8388608]{0:T(1024)(128)(4,1)} %bitcast.240), calls=%async_computation.1 | async-start | bytes 8388608
  357.6 8.9 %slice-start.3 = ((s8[8388608]{0:T(1024)(128)(4,1)}), s8[4194304]{0:T(1024)(128)(4,1)S(1)}, s32[]{:S(2)}) async-start(s8[8388608]{0:T(1024)(128)(4,1)} %bitcast.242), calls=%async_computation.4 | async-start | bytes 8388608
  357.6 9.0 %copy-start.6 = (bf16[6,64,2048]{2,1,0:T(8,128)(2,1)S(1)}, bf16[6,64,2048]{2,1,0:T(8,128)(2,1)}, u32[]{:S(2)}) copy-start(bf16[6,64,2048]{2,1,0:T(8,128)(2,1)} %get-tuple-element.23) | copy-start | bytes 4718596
  357.6 13.6 %slice-start.1 = ((s8[8388608]{0:T(1024)(128)(4,1)}), s8[4194304]{0:T(1024)(128)(4,1)S(1)}, s32[]{:S(2)}) async-start(s8[8388608]{0:T(1024)(128)(4,1)} %bitcast.240), calls=%async_computation.2 | async-start | bytes 8388608
  366.6 10.8 %slice-start.4 = ((s8[8388608]{0:T(1024)(128)(4,1)}), s8[4194304]{0:T(1024)(128)(4,1)S(1)}, s32[]{:S(2)}) async-start(s8[8388608]{0:T(1024)(128)(4,1)} %bitcast.244), calls=%async_computation.5 | async-start | bytes 8388608
  366.6 14.1 %slice-start.6 = ((s8[8388608]{0:T(1024)(128)(4,1)}), s8[4194304]{0:T(1024)(128)(4,1)S(1)}, s32[]{:S(2)}) async-start(s8[8388608]{0:T(1024)(128)(4,1)} %bitcast.246), calls=%async_computation.7 | async-start | bytes 8388608
  371.3 9.5 %slice-start.7 = ((s8[8388608]{0:T(1024)(128)(4,1)}), s8[4194304]{0:T(1024)(128)(4,1)S(1)}, s32[]{:S(2)}) async-start(s8[8388608]{0:T(1024)(128)(4,1)} %bitcast.246), calls=%async_computation.8 | async-start | bytes 8388608
  399.8 109.9 %copy-start.1 = (bf16[2,1,64,2048]{3,2,1,0:T(8,128)(2,1)S(1)}, bf16[2,1,64,2048]{3,2,1,0:T(8,128)(2,1)}, u32[]{:S(2)}) copy-start(bf16[2,1,64,2048]{3,2,1,0:T(8,128)(2,1)} %param.13) | copy-start | bytes 1572868
  399.8 109.9 %copy-start.44 = (f32[2048]{0:T(1024)S(1)}, f32[2048]{0:T(1024)}, u32[]{:S(2)}) copy-start(f32[2048]{0:T(1024)} %copy-done.43) | copy-start | bytes 24580
  399.8 109.9 %copy-start.48 = (f32[2,64]{1,0:T(2,128)S(1)}, f32[2,64]{1,0:T(2,128)}, u32[]{:S(2)}) copy-start(f32[2,64]{1,0:T(2,128)} %copy-done.47) | copy-start | bytes 1540
  399.8 109.9 %copy-start.50 = (f32[2,64]{1,0:T(2,128)S(1)}, f32[2,64]{1,0:T(2,128)}, u32[]{:S(2)}) copy-start(f32[2,64]{1,0:T(2,128)} %copy-done.49) | copy-start | bytes 1540
  399.8 112.9 %copy-start.24 = (bf16[2,1,64,2048]{3,2,1,0:T(8,128)(2,1)S(1)}, bf16[2,1,64,2048]{3,2,1,0:T(8,128)(2,1)}, u32[]{:S(2)}) copy-start(bf16[2,1,64,2048]{3,2,1,0:T(8,128)(2,1)} %param.14) | copy-start | bytes 1572868
  (46 other events, 186.7 us)
Sparse Core Ops, SparseCore 0:
  517.2 128.5 all-reduce.19
